TPU v7x, 256 devices: a whole 4x4x8 slice. The times are simulated.
256 devices in a mesh: cache: 64 (over x, z, core), section: 4 (over y).
Axes of the slice: x: 4, y: 4, z: 8, core: 2. Of those that a mesh axis runs over, the one named last changes fastest.
Arguments:
- hidden: bfloat16 [16384, 4096], P('cache'), may hold values from -24 to 24
- norm_gain: bfloat16 [4, 4096], P('section'), may hold values from 0.5 to 1.5
- own_kv: bfloat16 [4, 16384, 2048], P('section', 'cache'), may hold values from -128 to 128
- passage_kv: bfloat16 [4, 1024, 32, 2048], P('section', 'cache'), may hold values from -6 to 6
- retrieval: int32 [256, 8], P('cache'), may hold values from 0 to 1023, as said below
- passage_slot: int32 [1024], replicated, may hold values from 0 to 1023, as said below
Outputs:
- layers_out: bfloat16 [4, 16384, 4096], P('section', 'cache')
Inputs may be any that keep to these rules, and one draw needn't show every extreme that they name: `retrieval`: the 4 requests of index i of cache (requests i * 4 to (i + 1) * 4 - 1) name 32 different passages; at most 2 of them are stored on one index of cache (storage rows o * 16 to (o + 1) * 16 - 1 of passage_kv), exactly 2 on at least one. A permutation: passage p is row passage_slot[p] of passage_kv's second dimension.
All inputs are finite; a program needn't handle non-finite values.
Results may differ from a plain program's by a relative error of at most 0.0059.
Values may be sent and summed in bfloat16 or wider, within the bound.
A program may use at most 128 MiB of HBM per device.

v0:
```python
import functools

import jax
import jax.numpy as jnp
from jax import lax
from jax.experimental import pallas as pl
from jax.experimental.pallas import tpu as pltpu
from jax.sharding import PartitionSpec as P

D = 4096
QT = 64
PT = 32
NRET = 8
NX, NZ, NC, NY = 4, 8, 2, 4
PLANE = NX * NC
PASS_DEV = 16
REQ = 4
LAYERS = 4
CAP = 2
HALF = 256
PAIR = 512
WIDE = 1024
KEYS = 384
MESH = pl.DeviceIdType.MESH
STEPS = 2 * LAYERS
ONE = 256
CZS = (12, 14)
CX = 8
OWN = 64
KV_ROWS = NRET * PT + OWN


def mod(a, n):
    return lax.rem(a + n, n)


def where_am_i():
    cache = lax.axis_index("cache")
    y = lax.axis_index("section")
    c = lax.rem(cache, NC)
    z = lax.rem(cache // NC, NZ)
    x = cache // (NC * NZ)
    return cache, x, y, z, c


def cache_at(x, z, c):
    return (x * NZ + z) * NC + c


def greet_kernel(
    ids_ref,
    slot_ref,
    gain_ref,
    rows_out,
    gain_out,
    tab_out,
    mine,
    near,
    tile,
    far,
    fields,
    psend,
    precv,
    zsend,
    zrecv,
    gsend,
    grecv,
):
    cache, x, y, z, c = where_am_i()
    me = c * NX + x
    f32, bf16, i32 = jnp.float32, jnp.bfloat16, jnp.int32

    def plane_id(i):
        t = lax.rem(me + i, PLANE)
        return (cache_at(lax.rem(t, NX), z, t // NX), y)

    def z_id(i):
        return (cache_at(x, lax.rem(z + i, NZ), c), y)

    def y_id(i):
        return (cache, lax.rem(y + i, NY))

    def lanes(shape):
        return lax.broadcasted_iota(i32, shape, len(shape) - 1)

    def subs(shape):
        return lax.broadcasted_iota(i32, shape, len(shape) - 2)

    def mm(a, b):
        return jnp.dot(a.astype(bf16), b.astype(bf16), preferred_element_type=f32)

    barrier = pltpu.get_barrier_semaphore()
    for count, peer in ((PLANE, plane_id), (NZ, z_id), (NY, y_id)):
        for i in range(1, count):
            pl.semaphore_signal(barrier, inc=1, device_id=peer(i), device_id_type=MESH)

    ids = ids_ref[0:1, :]
    hit = (jnp.broadcast_to(ids % 128, (128, 128)) == subs((128, 128))).astype(f32)
    high = mm((slot_ref[...] // 32).astype(f32), hit)
    low = mm((slot_ref[...] % 32).astype(f32), hit)
    pick = jnp.broadcast_to(ids // 128, (8, 128)) == subs((8, 128))
    found = jnp.sum(jnp.where(pick, high * 32.0 + low, 0.0), axis=0, keepdims=True)
    found = jnp.where(lanes((1, 128)) // 32 == lax.rem(me, 4), found, 0.0)
    mine[...] = jnp.broadcast_to(found, (8, 128)).astype(i32)
    for i in range(32):
        gain_out[y, i : i + 1, :] = gain_ref[:, i * 128 : (i + 1) * 128].astype(f32)

    pl.semaphore_wait(barrier, PLANE + NZ + NY - 3)
    first, second, third = [], [], []
    for i in range(1, PLANE):
        first.append(
            pltpu.make_async_remote_copy(
                src_ref=mine,
                dst_ref=near.at[me],
                send_sem=psend.at[i],
                recv_sem=precv.at[i],
                device_id=plane_id(i),
                device_id_type=MESH,
            )
        )
    for i in range(1, NY):
        second.append(
            pltpu.make_async_remote_copy(
                src_ref=gain_out.at[y],
                dst_ref=gain_out.at[y],
                send_sem=gsend.at[i],
                recv_sem=grecv.at[i],
                device_id=y_id(i),
                device_id_type=MESH,
            )
        )
    for copy in first + second:
        copy.start()
    near[me] = mine[...]
    for copy in first:
        copy.wait()
    row = subs((8, 128))
    tile[...] = jnp.where(row == 0, near[0] + near[1] + near[2] + near[3], 0) + jnp.where(
        row == 1, near[4] + near[5] + near[6] + near[7], 0
    )
    for i in range(1, NZ):
        third.append(
            pltpu.make_async_remote_copy(
                src_ref=tile,
                dst_ref=far.at[z],
                send_sem=zsend.at[i],
                recv_sem=zrecv.at[i],
                device_id=z_id(i),
                device_id_type=MESH,
            )
        )
    for copy in third:
        copy.start()
    far[z] = tile[...]
    for copy in third:
        copy.wait()
    for i in range(NZ):
        rows_out[2 * i : 2 * i + 2, :] = far[i, 0:2, :]

    rows = rows_out[...]
    owner = rows // PASS_DEV
    inside = rows % PASS_DEV
    plane = (owner // NC) % NZ
    o8 = (owner % NC) * NX + owner // (NZ * NC)
    stripe = (inside + o8) % PLANE
    place = o8 * 2 + inside // PLANE
    group = plane * PLANE + stripe
    chip = stripe % NX

    wide = (128, 128)
    same = (subs(wide) // 32 == lanes(wide) // 32) & (subs(wide) < lanes(wide))
    rank = jnp.zeros((2 * NZ, 128), f32)
    for v in range(NX):
        here = (chip == v).astype(f32)
        rank = rank + here * mm(here, same.astype(f32))
    rank = rank.astype(i32)
    fields[0] = group
    fields[1] = place
    fields[2] = chip
    fields[3] = rank

    groups = NZ * PLANE
    count = jnp.zeros((PASS_DEV, groups), f32)
    for i in range(2 * NZ):
        in_group = jnp.broadcast_to(group[i : i + 1], (groups, 128)) == subs((groups, 128))
        in_place = jnp.broadcast_to(place[i : i + 1], (PASS_DEV, 128)) == subs((PASS_DEV, 128))
        count = count + lax.dot_general(
            in_place.astype(f32).astype(bf16),
            in_group.astype(f32).astype(bf16),
            (((1,), (1,)), ((), ())),
            preferred_element_type=f32,
        )
    need = (count > 0.5).astype(f32)
    square = (PASS_DEV, PASS_DEV)
    before = mm((lanes(square) < subs(square)).astype(f32), need)

    def one_max(value):
        return jnp.max(jnp.max(value, axis=1, keepdims=True), axis=0, keepdims=True)

    most_z = one_max(jnp.sum(need, axis=0, keepdims=True)).astype(i32)
    most_x = one_max(rank) + 1

    ours = (lanes((PASS_DEV, groups)) == z * PLANE + me).astype(f32)
    my_need = jnp.sum(need * ours, axis=1, keepdims=True)
    my_before = jnp.sum(before * ours, axis=1, keepdims=True).astype(i32)
    hit = (my_before == lanes((PASS_DEV, 128))) & (my_need > 0.5)
    csel = jnp.sum(jnp.where(hit, subs((PASS_DEV, 128)), 0), axis=0, keepdims=True)
    tab_out[0:8, :] = jnp.broadcast_to(csel, (8, 128))

    block = (subs(wide) // 32 == lanes(wide)).astype(f32)
    for half in range(2):
        at = pl.ds(2 * z + half, 1)
        g, a, b, k = fields[0, at, :], fields[1, at, :], fields[2, at, :], fields[3, at, :]
        in_group = jnp.broadcast_to(g, (groups, 128)) == subs((groups, 128))
        in_place = jnp.broadcast_to(a, (PASS_DEV, 128)) == subs((PASS_DEV, 128))
        spot = mm(before, in_group.astype(f32)) * in_place.astype(f32)
        spot = jnp.sum(spot, axis=0, keepdims=True)
        core = (g % PLANE) // NX
        where = ((core * NZ + g // PLANE) * CZS[-1]).astype(f32) + jnp.minimum(spot, CZS[-1] - 1.0)
        key = jnp.where((b == x) & (k % NC == c), k // NC, -1)
        hit = jnp.broadcast_to(key, (CX, 128)) == subs((CX, 128))
        chosen = jnp.where(hit, jnp.broadcast_to(where, (CX, 128)), 0.0)
        tab_out[8 + 8 * half : 16 + 8 * half, :] = mm(chosen, block).astype(i32)
        slot = ((k % NC) * NX + b) * CX + jnp.minimum(k // NC, CX - 1)
        tab_out[24 + half : 25 + half, :] = slot
    tab_out[26:27, :] = jnp.broadcast_to(most_z, (1, 128))
    tab_out[27:28, :] = jnp.broadcast_to(most_x, (1, 128))
    tab_out[28:32, :] = jnp.zeros((4, 128), i32)
    for copy in second:
        copy.wait()


def greet(ids, slot, gain):
    vmem = pl.BlockSpec(memory_space=pltpu.VMEM)
    dma = pltpu.SemaphoreType.DMA
    return pl.pallas_call(
        greet_kernel,
        out_shape=(
            jax.ShapeDtypeStruct((2 * NZ, 128), jnp.int32),
            jax.ShapeDtypeStruct((NY, 32, 128), jnp.float32),
            jax.ShapeDtypeStruct((32, 128), jnp.int32),
        ),
        in_specs=[vmem, vmem, vmem],
        out_specs=(vmem, vmem, vmem),
        scratch_shapes=[
            pltpu.VMEM((8, 128), jnp.int32),
            pltpu.VMEM((PLANE, 8, 128), jnp.int32),
            pltpu.VMEM((8, 128), jnp.int32),
            pltpu.VMEM((NZ, 8, 128), jnp.int32),
            pltpu.VMEM((4, 2 * NZ, 128), jnp.int32),
            dma((PLANE,)),
            dma((PLANE,)),
            dma((NZ,)),
            dma((NZ,)),
            dma((NY,)),
            dma((NY,)),
        ],
        compiler_params=pltpu.CompilerParams(collective_id=0, has_side_effects=True),
        name="greet",
    )(ids, slot, gain)


def fast_kernel(
    cz, store, own_in, hid, gain, tab, out, ybuf, send, kvs, own, state, staged, gains, rs,
    ssq, box, packed, ysend, yrecv, osend, orecv, local, ssend, srecv, csend, crecv, zsend, zrecv, xsend, xrecv,
    qsend, qrecv, outsend, outrecv, outlocal, *many
):
    strips, pools, recvs = many[:STEPS], many[STEPS : 2 * STEPS], many[2 * STEPS :]
    cache, x, y, z, c = where_am_i()
    me = c * NX + x
    scale = 1.4426950408889634 / 128**0.5

    def plane_id(t):
        return (cache_at(lax.rem(t, NX), z, t // NX), y)

    def z_id(dz):
        return (cache_at(x, mod(z + dz, NZ), c), y)

    def y_id(s):
        return (cache, s)

    def step_of(i, s):
        return jnp.where(i == 2 * s, 0, jnp.where(i < 2 * s, i + 1, i))

    def part_of(q):
        return 2 * y if q == 0 else jnp.where(q - 1 < 2 * y, q - 1, q)

    barrier = pltpu.get_barrier_semaphore()
    for i in range(1, PLANE):
        pl.semaphore_signal(
            barrier, inc=1, device_id=plane_id(lax.rem(me + i, PLANE)), device_id_type=MESH
        )
    for i in range(1, NY):
        pl.semaphore_signal(
            barrier, inc=1, device_id=y_id(lax.rem(y + i, NY)), device_id_type=MESH
        )
    for dz in (1, -1):
        pl.semaphore_signal(barrier, inc=1, device_id=z_id(dz), device_id_type=MESH)
    pl.semaphore_wait(barrier, PLANE + NY)

    def local_copies():
        made = []
        for j in range(2):
            for part in range(2):
                cols = pl.ds(pl.multiple_of(part * 1024 + y * HALF + j * 128, 128), 128)
                made.append(
                    pltpu.make_async_copy(
                        store.at[:, :, :, cols],
                        ybuf.at[step_of(2 * y + j, y), :, :, :, pl.ds(part * 128, 128)],
                        local.at[2 * j + part],
                    )
                )
        for part in range(2):
            cols = pl.ds(pl.multiple_of(part * 1024 + y * HALF, HALF), HALF)
            made.append(
                pltpu.make_async_copy(
                    own_in.at[:, cols], own.at[y, :, pl.ds(part * HALF, HALF)], local.at[4 + part]
                )
            )
        return made

    def pack_copies(i, j):
        s = lax.rem(y + i, NY)
        made = []
        for part in range(2):
            cols = pl.ds(pl.multiple_of(part * 1024 + s * HALF + j * 128, 128), 128)
            made.append(
                pltpu.make_async_copy(
                    store.at[:, :, :, cols],
                    box.at[i - 1, j, :, :, :, pl.ds(part * 128, 128)],
                    packed.at[i, j, part],
                )
            )
        return made

    def scatter_copy(i, j):
        s = lax.rem(y + i, NY)
        q = step_of(2 * y + j, s)
        return pltpu.make_async_remote_copy(
            src_ref=box.at[i - 1, j],
            dst_ref=ybuf.at[q],
            send_sem=ysend.at[i, j],
            recv_sem=yrecv.at[q],
            device_id=y_id(s),
            device_id_type=MESH,
        )

    def own_scatter(i):
        s = lax.rem(y + i, NY)
        made = []
        for part in range(2):
            cols = pl.ds(pl.multiple_of(part * 1024 + s * HALF, HALF), HALF)
            made.append(
                pltpu.make_async_remote_copy(
                    src_ref=own_in.at[:, cols],
                    dst_ref=own.at[y, :, pl.ds(part * HALF, HALF)],
                    send_sem=osend.at[i, part],
                    recv_sem=orecv.at[y, part],
                    device_id=y_id(s),
                    device_id_type=MESH,
                )
            )
        return made

    def stripe(q):
        def push(i, _):
            t = lax.rem(me + i, PLANE)
            pltpu.make_async_remote_copy(
                src_ref=ybuf.at[q, :, mod(t - me, PLANE)],
                dst_ref=strips[q].at[pl.ds(me * 2, 2)],
                send_sem=ssend.at[q],
                recv_sem=srecv.at[q],
                device_id=plane_id(t),
                device_id_type=MESH,
            ).start()
            return 0

        strips[q][pl.ds(me * 2, 2)] = ybuf[q, :, 0]
        lax.fori_loop(1, PLANE, push, 0)

    def z_ref(q, plane, half):
        at = (c * NZ + plane) * CZS[-1]
        if half == 0:
            return pools[q].at[pl.ds(at, cz - cz // 2)]
        return pools[q].at[pl.ds(at + cz - cz // 2, cz // 2)]

    def z_copy(q, up, half, hop):
        where = z_ref(q, mod(z - (hop - 1), NZ) if up else mod(z + (hop - 1), NZ), half)
        return pltpu.make_async_remote_copy(
            src_ref=where,
            dst_ref=where,
            send_sem=zsend.at[q, int(up), half, hop - 1],
            recv_sem=zrecv.at[q, int(up), half, hop - 1],
            device_id=z_id(1 if up else -1),
            device_id_type=MESH,
        )

    def z_arrival(q, up, half, hop):
        where = z_ref(q, mod(z - hop, NZ) if up else mod(z + hop, NZ), half)
        return pltpu.make_async_remote_copy(
            src_ref=where,
            dst_ref=where,
            send_sem=zsend.at[q, int(up), half, hop - 1],
            recv_sem=zrecv.at[q, int(up), half, hop - 1],
            device_id=z_id(1 if up else -1),
            device_id_type=MESH,
        )

    def hops(up, half):
        return 4 if bool(up) == (half == 0) else 3

    def share(where, q):
        pltpu.make_async_remote_copy(
            src_ref=where,
            dst_ref=where,
            send_sem=csend.at[q],
            recv_sem=crecv.at[q],
            device_id=(cache_at(x, z, 1 - c), y),
            device_id_type=MESH,
        ).start()

    def compact(q):
        what = strips[q].at[pl.ds(0, 2 * PLANE - 2)]
        pltpu.make_async_copy(what, what, srecv.at[q]).wait()
        for i in range(cz):
            pools[q][(c * NZ + z) * CZS[-1] + i] = strips[q][tab[0, i]]
        for half in range(2):
            for up in (True, False):
                z_copy(q, up, half, 1).start()
        share(pools[q].at[pl.ds((c * NZ + z) * CZS[-1], cz)], q)

    def choose(q):
        par = q % 2
        what = pools[q].at[pl.ds(0, NZ * cz)]
        pltpu.make_async_copy(what, what, crecv.at[q]).wait()
        if q >= 2:
            x_sent(q - 2)

        def fill(t, _):
            for i in range(CX):
                send[par, t, i] = pools[q][tab[8 + 8 * (t // 4) + i, lax.rem(t, 4)]]
            return 0

        lax.fori_loop(0, PLANE, fill, 0)
        recvs[q][pl.ds(me * CX, CX)] = send[par, me]

        def push(i, _):
            t = lax.rem(me + i, PLANE)
            pltpu.make_async_remote_copy(
                src_ref=send.at[par, t],
                dst_ref=recvs[q].at[pl.ds(me * CX, CX)],
                send_sem=xsend.at[q],
                recv_sem=xrecv.at[q],
                device_id=plane_id(t),
                device_id_type=MESH,
            ).start()
            return 0

        lax.fori_loop(1, PLANE, push, 0)

    def x_sent(q):
        what = send.at[q % 2, pl.ds(0, PLANE - 1)]
        pltpu.make_async_copy(what, what, xsend.at[q]).wait()

    def assemble(q):
        what = recvs[q].at[pl.ds(0, (PLANE - 1) * CX)]
        pltpu.make_async_copy(what, what, xrecv.at[q]).wait()
        part = part_of(q)

        def one(r, _):
            for n in range(NRET):
                at = tab[24 + me // 4, lax.rem(me, 4) * 32 + r * NRET + n]
                kvs[part, r, n * PT : (n + 1) * PT] = recvs[q][at]
            return 0

        lax.fori_loop(0, REQ, one, 0)

    def y_arrived(q):
        what = ybuf.at[q]
        pltpu.make_async_copy(what, what, yrecv.at[q]).wait()

    krow = lax.broadcasted_iota(jnp.int32, (OWN, 4 * QT), 0)
    qcol = lax.rem(lax.broadcasted_iota(jnp.int32, (OWN, 4 * QT), 1), QT)

    def before_layer(layer):
        @pl.when(layer != y)
        def _():
            for part in range(2):
                what = own.at[layer, :, pl.ds(part * HALF, HALF)]
                pltpu.make_async_copy(what, what, orecv.at[layer, part]).wait()

        if layer > 0:
            what = ssq.at[layer - 1, pl.ds(0, NY - 1)]
            pltpu.make_async_copy(what, what, qrecv.at[layer - 1]).wait()
            total = ssq[layer - 1, 0] + ssq[layer - 1, 1] + ssq[layer - 1, 2] + ssq[layer - 1, 3]
            total = total + pltpu.roll(total, QT, 1)
            total = total + pltpu.roll(total, 2 * QT, 1)
            rs[...] = lax.rsqrt(total * (1.0 / D) + 1e-05)

    def attend(layer, r, heads_of):
        rows = pl.ds(pl.multiple_of(r * QT, QT), QT)
        causal = krow <= qcol
        squares = jnp.zeros((1, 4 * QT), jnp.float32)
        for j in heads_of:
            part = 2 * layer + j
            wide = state[r, j].astype(jnp.float32)
            query = (wide * rs[pl.ds(r, 1), :] * gains[layer, j]).astype(jnp.bfloat16)
            far_keys = kvs[part, r, :, 0:128]
            far_vals = kvs[part, r, :, 128:256]
            near_keys = own[layer, rows, j * 128 : (j + 1) * 128]
            near_vals = own[layer, rows, HALF + j * 128 : HALF + (j + 1) * 128]
            far = jnp.dot(far_keys, query, preferred_element_type=jnp.float32)
            near = jnp.dot(near_keys, query, preferred_element_type=jnp.float32)
            near = jnp.where(causal, near, -jnp.inf)
            top = jnp.maximum(
                jnp.max(far, axis=0, keepdims=True), jnp.max(near, axis=0, keepdims=True)
            )
            far = jnp.exp2((far - top) * scale)
            near = jnp.exp2((near - top) * scale)
            total = jnp.sum(far, axis=0, keepdims=True) + jnp.sum(near, axis=0, keepdims=True)
            total = 1.0 / total
            far = (far * total).astype(jnp.bfloat16)
            near = (near * total).astype(jnp.bfloat16)
            first = (((0,), (0,)), ((), ()))
            mixed = lax.dot_general(far_vals, far, first, preferred_element_type=jnp.float32)
            mixed = mixed + lax.dot_general(
                near_vals, near, first, preferred_element_type=jnp.float32
            )
            new = (wide + mixed).astype(jnp.bfloat16)
            state[r, j] = new
            turned = new.T
            for g in range(4):
                h = 4 * j + g
                staged[layer, rows, h * 128 : (h + 1) * 128] = turned[g * QT : (g + 1) * QT]
            new = new.astype(jnp.float32)
            squares = squares + jnp.sum(new * new, axis=0, keepdims=True)
        if layer < LAYERS - 1:
            ssq[layer, y, pl.ds(r, 1), :] = squares
        width = PAIR * len(heads_of)
        cols = pl.ds(pl.multiple_of(y * WIDE + heads_of[0] * PAIR, PAIR), width)
        made = staged.at[layer, rows, pl.ds(heads_of[0] * PAIR, width)]

        @pl.when(layer == y)
        def _():
            pltpu.make_async_copy(made, out.at[rows, cols], outlocal).start()

        @pl.when(layer != y)
        def _():
            pltpu.make_async_remote_copy(
                src_ref=made,
                dst_ref=out.at[rows, cols],
                send_sem=outsend.at[layer],
                recv_sem=outrecv,
                device_id=y_id(layer),
                device_id_type=MESH,
            ).start()

    def after_layer(layer):
        for i in range(1, NY):
            pltpu.make_async_remote_copy(
                src_ref=ssq.at[layer, y],
                dst_ref=ssq.at[layer, y],
                send_sem=qsend.at[layer, i],
                recv_sem=qrecv.at[layer],
                device_id=y_id(lax.rem(y + i, NY)),
                device_id_type=MESH,
            ).start()

    def attend_rows(layer, first, count, together, heads_of=(0, 1)):
        def body(i, _):
            for u in range(together):
                attend(layer, first + i * together + u, heads_of)
            return 0

        lax.fori_loop(0, count // together, body, 0)

    own_copies = local_copies()
    for copy in own_copies[:2]:
        copy.start()
    packs = [(i, j, pack_copies(i, j)) for j in range(2) for i in (1, 3, 2)]
    for i, j, copies in packs[:3]:
        for copy in copies:
            copy.start()
    for copy in own_copies[2:]:
        copy.start()
    for i, j, copies in packs[3:]:
        for copy in copies:
            copy.start()
    own_copies[0].wait()
    own_copies[1].wait()
    stripe(0)
    for i, j, copies in packs:
        for copy in copies:
            copy.wait()

    def scatter(first, last):
        @pl.when((y >= first) & (y <= last))
        def _():
            for j in range(2):
                for i in (1, 3, 2):
                    scatter_copy(i, j).start()

    def scatter_own():
        for i in (1, 3, 2):
            for copy in own_scatter(i):
                copy.start()

    scatter(0, 1)
    compact(0)

    for layer in range(LAYERS - 1):
        ssq[layer, y] = jnp.zeros((8, 4 * QT), jnp.float32)
    mean_sq = jnp.zeros((REQ * QT, 1), jnp.float32)
    for i in range(8):
        wide = hid[:, i * 512 : (i + 1) * 512].astype(jnp.float32)
        mean_sq = mean_sq + jnp.sum(wide * wide, axis=-1, keepdims=True)
    mean_sq = jnp.broadcast_to(mean_sq * (1.0 / D), (REQ * QT, 128)).T
    mean_sq = lax.rsqrt(mean_sq + 1e-05)
    for r in range(REQ):
        part = mean_sq[0:1, r * QT : (r + 1) * QT]
        rs[r : r + 1, :] = jnp.concatenate([part] * 4, axis=1)
    rs[REQ:, :] = jnp.zeros((8 - REQ, 4 * QT), jnp.float32)
    for j in range(2):
        for r in range(REQ):
            heads = []
            for g in range(4):
                cols = pl.ds(pl.multiple_of(y * WIDE + (4 * j + g) * 128, 128), 128)
                heads.append(hid[r * QT : (r + 1) * QT, cols])
            state[r, j] = jnp.concatenate(heads, axis=0).T
        for layer in range(LAYERS):
            heads = []
            for g in range(4):
                at = gain[layer, pl.ds(y * 8 + 4 * j + g, 1), :]
                heads.append(jnp.broadcast_to(at, (QT, 128)))
            gains[layer, j] = jnp.concatenate(heads, axis=0).T

    def arrived_from_y(q):
        part = part_of(q)

        @pl.when(part != 2 * y + 1)
        def _():
            y_arrived(q)

    for copy in own_copies[2:]:
        copy.wait()
    arrived_from_y(1)
    stripe(1)
    todo = {}

    def later(slot, work):
        todo.setdefault(slot, []).append(work)

    later(0, lambda: scatter(2, 2))
    later(1, lambda: scatter(3, 3))
    later(3, scatter_own)

    for q in range(1, STEPS):
        if q >= 2:
            later(q - 1, lambda q=q: (arrived_from_y(q), stripe(q)))
        later(2 * q - 1, lambda q=q: compact(q))
    for q in range(STEPS):
        later(2 * q + 4, lambda q=q: choose(q))
    for q in range(STEPS - 1):
        later(2 * q + 6, lambda q=q: assemble(q))
    for layer in range(2):
        later(4 * layer + 10, lambda layer=layer: before_layer(layer))
        for half in range(2):
            later(
                4 * layer + 10 + 2 * half,
                lambda layer=layer, half=half: attend_rows(layer, 2 * half, 2, 1),
            )
        later(4 * layer + 12, lambda layer=layer: after_layer(layer))

    for slot in range(2 * STEPS + 3):
        for q in range(STEPS):
            hop = slot - 2 * q + 1
            if not 1 <= hop <= 4:
                continue
            for half in range(2):
                for up in (True, False):
                    if hop <= hops(up, half):
                        z_arrival(q, up, half, hop).wait_recv()
                        if hop < hops(up, half):
                            z_copy(q, up, half, hop + 1).start()
                        plane = mod(z - hop, NZ) if up else mod(z + hop, NZ)
                        share(z_ref(q, plane, half), q)
        for work in todo.get(slot, ()):
            work()

    before_layer(2)
    attend_rows(2, 0, REQ, 2)
    after_layer(2)
    before_layer(3)
    attend_rows(3, 0, REQ, 2, (0,))
    assemble(STEPS - 1)
    attend_rows(3, 0, REQ, 2, (1,))

    x_sent(STEPS - 2)
    x_sent(STEPS - 1)
    for q in range(STEPS):
        what = strips[q].at[pl.ds(0, 2 * PLANE - 2)]
        pltpu.make_async_copy(what, what, ssend.at[q]).wait()
        what = pools[q].at[pl.ds(0, NZ * cz)]
        pltpu.make_async_copy(what, what, csend.at[q]).wait()
        for up in (True, False):
            for half in range(2):
                for hop in range(1, hops(up, half) + 1):
                    z_copy(q, up, half, hop).wait_send()
    for i in range(1, NY):
        for j in range(2):
            scatter_copy(i, j).wait_send()
        for copy in own_scatter(i):
            copy.wait_send()
        for layer in range(LAYERS - 1):
            what = ssq.at[layer, y]
            pltpu.make_async_copy(what, what, qsend.at[layer, i]).wait()
    for layer in range(LAYERS):

        @pl.when(layer != y)
        def _():
            what = staged.at[layer]
            pltpu.make_async_copy(what, what, outsend.at[layer]).wait()

    what = out.at[:, pl.ds(0, 3 * WIDE)]
    pltpu.make_async_copy(what, what, outrecv).wait()
    what = out.at[:, pl.ds(0, WIDE)]
    pltpu.make_async_copy(what, what, outlocal).wait()


def fast_attend(cz, collective_id, store, own, hidden, gain, tab):
    vmem = pl.BlockSpec(memory_space=pltpu.VMEM)
    smem = pl.BlockSpec(memory_space=pltpu.SMEM)
    hbm = pl.BlockSpec(memory_space=pl.ANY)
    bf16 = jnp.bfloat16
    dma = pltpu.SemaphoreType.DMA
    return pl.pallas_call(
        functools.partial(fast_kernel, cz),
        out_shape=jax.ShapeDtypeStruct((REQ * QT, D), bf16),
        in_specs=[hbm, hbm, vmem, vmem, smem],
        out_specs=hbm,
        scratch_shapes=[
            pltpu.VMEM((STEPS, 2, PLANE, PT, ONE), bf16),
            pltpu.VMEM((2, PLANE, CX, PT, ONE), bf16),
            pltpu.VMEM((STEPS, REQ, NRET * PT, ONE), bf16),
            pltpu.VMEM((LAYERS, REQ * QT, PAIR), bf16),
            pltpu.VMEM((REQ, 2, 128, 4 * QT), bf16),
            pltpu.VMEM((LAYERS, REQ * QT, WIDE), bf16),
            pltpu.VMEM((LAYERS, 2, 128, 4 * QT), jnp.float32),
            pltpu.VMEM((8, 4 * QT), jnp.float32),
            pltpu.VMEM((LAYERS - 1, NY, 8, 4 * QT), jnp.float32),
            pltpu.VMEM((NY - 1, 2, 2, PLANE, PT, ONE), bf16),
            dma((NY, 2, 2)),
            dma((NY, 2)),
            dma((STEPS,)),
            dma((NY, 2)),
            dma((LAYERS, 2)),
            dma((6,)),
            dma((STEPS,)),
            dma((STEPS,)),
            dma((STEPS,)),
            dma((STEPS,)),
            dma((STEPS, 2, 2, 4)),
            dma((STEPS, 2, 2, 4)),
            dma((STEPS,)),
            dma((STEPS,)),
            dma((LAYERS - 1, NY)),
            dma((LAYERS - 1,)),
            dma((LAYERS,)),
            dma(()),
            dma(()),
        ]
        + [pltpu.VMEM((PLANE * 2, PT, ONE), bf16)] * STEPS
        + [pltpu.VMEM((NC * NZ * CZS[-1], PT, ONE), bf16)] * STEPS
        + [pltpu.VMEM((PLANE * CX, PT, ONE), bf16)] * STEPS,
        compiler_params=pltpu.CompilerParams(
            collective_id=collective_id, has_side_effects=True, vmem_limit_bytes=60 * 1024 * 1024
        ),
        name="fast_attend_" + str(cz),
    )(store, own, hidden, gain, tab)


def general_kernel(
    store,
    own_in,
    hid,
    gain,
    sel,
    slots,
    out,
    pool,
    recv,
    send,
    rstage,
    stage,
    own,
    kv,
    state,
    rs,
    ssq,
    ysend,
    yrecv,
    osend,
    orecv,
    local,
    zsend,
    zrecv,
    xsend,
    xrecv,
    qsend,
    qrecv,
    outsend,
    outrecv,
    outlocal,
):
    cache, x, y, z, c = where_am_i()
    me = x * NC + c

    def plane_id(t):
        return (cache_at(t // NC, z, lax.rem(t, NC)), y)

    def z_id(dz):
        return (cache_at(x, mod(z + dz, NZ), c), y)

    def y_id(s):
        return (cache, s)

    def step_of(layer, s):
        return jnp.where(layer == s, 0, jnp.where(layer < s, layer + 1, layer))

    barrier = pltpu.get_barrier_semaphore()
    for i in range(1, PLANE):
        pl.semaphore_signal(
            barrier, inc=1, device_id=plane_id(lax.rem(me + i, PLANE)), device_id_type=MESH
        )
    for i in range(1, NY):
        pl.semaphore_signal(
            barrier, inc=1, device_id=y_id(lax.rem(y + i, NY)), device_id_type=MESH
        )
    for dz in (1, -1):
        pl.semaphore_signal(barrier, inc=1, device_id=z_id(dz), device_id_type=MESH)
    pl.semaphore_wait(barrier, PLANE + NY)

    def local_copies():
        made = []
        for part in range(2):
            cols = pl.ds(pl.multiple_of(part * 1024 + y * HALF, HALF), HALF)
            half = pl.ds(part * HALF, HALF)
            made.append(
                pltpu.make_async_copy(
                    store.at[:, :, cols], pool.at[0, z, :, :, half], local.at[part]
                )
            )
            made.append(
                pltpu.make_async_copy(
                    own_in.at[:, cols], own.at[y, :, half], local.at[2 + part]
                )
            )
        return made

    def scatter_copies(i):
        s = lax.rem(y + i, NY)
        made = []
        for part in range(2):
            cols = pl.ds(pl.multiple_of(part * 1024 + s * HALF, HALF), HALF)
            half = pl.ds(part * HALF, HALF)
            made.append(
                pltpu.make_async_remote_copy(
                    src_ref=store.at[:, :, cols],
                    dst_ref=pool.at[step_of(y, s), z, :, :, half],
                    send_sem=ysend.at[i, part],
                    recv_sem=yrecv.at[step_of(y, s), part],
                    device_id=y_id(s),
                    device_id_type=MESH,
                )
            )
            made.append(
                pltpu.make_async_remote_copy(
                    src_ref=own_in.at[:, cols],
                    dst_ref=own.at[y, :, half],
                    send_sem=osend.at[i, part],
                    recv_sem=orecv.at[y, part],
                    device_id=y_id(s),
                    device_id_type=MESH,
                )
            )
        return made

    for copy in local_copies():
        copy.start()
    for i in (1, 3, 2):
        for copy in scatter_copies(i):
            copy.start()

    def z_copy(k, up, half, hop):
        plane = mod(z - (hop - 1), NZ) if up else mod(z + (hop - 1), NZ)
        rows = pl.ds(half * 8, 8)
        where = pool.at[k, plane, rows]
        return pltpu.make_async_remote_copy(
            src_ref=where,
            dst_ref=where,
            send_sem=zsend.at[k, int(up), half, hop - 1],
            recv_sem=zrecv.at[k, int(up), half, hop - 1],
            device_id=z_id(1 if up else -1),
            device_id_type=MESH,
        )

    def z_arrival(k, up, half, hop):
        plane = mod(z - hop, NZ) if up else mod(z + hop, NZ)
        where = pool.at[k, plane, pl.ds(half * 8, 8)]
        return pltpu.make_async_remote_copy(
            src_ref=where,
            dst_ref=where,
            send_sem=zsend.at[k, int(up), half, hop - 1],
            recv_sem=zrecv.at[k, int(up), half, hop - 1],
            device_id=z_id(1 if up else -1),
            device_id_type=MESH,
        )

    def hops(up, half):
        return 4 if bool(up) == (half == 0) else 3

    def z_first(k):
        for half in range(2):
            for up in (True, False):
                z_copy(k, up, half, 1).start()

    def choose(k, plane):
        par = lax.rem(k, 2)
        stage[...] = pool[k, plane]

        def fill(t, _):
            for r in range(CAP):
                send[par, plane, t, r] = stage[sel[plane, t * CAP + r]]
            return 0

        lax.fori_loop(0, PLANE, fill, 0)
        recv[k, me, plane] = send[par, plane, me]

        def push(i, _):
            t = lax.rem(me + i, PLANE)
            pltpu.make_async_remote_copy(
                src_ref=send.at[par, plane, t],
                dst_ref=recv.at[k, me, plane],
                send_sem=xsend.at[k],
                recv_sem=xrecv.at[k],
                device_id=plane_id(t),
                device_id_type=MESH,
            ).start()
            return 0

        lax.fori_loop(1, PLANE, push, 0)

    def x_sent(k):
        what = send.at[lax.rem(k, 2), :, pl.ds(0, PLANE - 1)]
        pltpu.make_async_copy(what, what, xsend.at[k]).wait()

    def x_arrived(k):
        what = recv.at[k, pl.ds(0, PLANE - 1)]
        pltpu.make_async_copy(what, what, xrecv.at[k]).wait()

    def y_arrived(k):
        for part in range(2):
            what = pool.at[k, z, :, :, pl.ds(part * HALF, HALF)]
            pltpu.make_async_copy(what, what, yrecv.at[k, part]).wait()

    def attend(layer):
        k = step_of(layer, y)

        def lift(i, _):
            rstage[pl.ds(i * 16, 16)] = recv[k, i].reshape(16, PT, PAIR)
            return 0

        lax.fori_loop(0, PLANE, lift, 0)

        @pl.when(layer != y)
        def _():
            for part in range(2):
                what = own.at[layer, :, pl.ds(part * HALF, HALF)]
                pltpu.make_async_copy(what, what, orecv.at[layer, part]).wait()

        if layer > 0:
            what = ssq.at[layer - 1, pl.ds(0, NY - 1)]
            pltpu.make_async_copy(what, what, qrecv.at[layer - 1]).wait()
            total = ssq[layer - 1, 0] + ssq[layer - 1, 1] + ssq[layer - 1, 2] + ssq[layer - 1, 3]
            total = jnp.broadcast_to(total[0:1], (128, 256)).T
            rs[...] = lax.rsqrt(total * (1.0 / D) + 1e-05)

        row = lax.rem(lax.broadcasted_iota(jnp.int32, (4 * QT, KEYS), 0), QT)
        col = lax.broadcasted_iota(jnp.int32, (4 * QT, KEYS), 1)
        seen = (col < NRET * PT + 1 + row)

        def one(r, _):
            rows = pl.ds(pl.multiple_of(r * QT, QT), QT)
            for n in range(NRET):
                kv[n * PT : (n + 1) * PT] = rstage[slots[r * NRET + n]]
            kv[NRET * PT : NRET * PT + QT] = own[layer, rows]
            if layer == 0:
                before = hid[rows, pl.ds(pl.multiple_of(y * WIDE, WIDE), WIDE)]
            else:
                before = state[layer - 1, rows]
            wide = before.astype(jnp.float32)
            query = (wide * rs[rows, 0:1] * gain[layer : layer + 1, :]).astype(jnp.bfloat16)
            squares = jnp.zeros((QT, 128), jnp.float32)
            for j in range(2):
                heads = [4 * j + g for g in range(4)]
                qj = jnp.concatenate([query[:, h * 128 : (h + 1) * 128] for h in heads], axis=0)
                keys = kv[:, j * 128 : (j + 1) * 128]
                vals = kv[:, HALF + j * 128 : HALF + (j + 1) * 128]
                score = lax.dot_general(
                    qj, keys, (((1,), (1,)), ((), ())), preferred_element_type=jnp.float32
                )
                score = jnp.where(seen, score * (1.0 / 128**0.5), -jnp.inf)
                top = jnp.max(score, axis=-1, keepdims=True)
                expd = jnp.exp(score - top)
                total = jnp.sum(expd, axis=-1, keepdims=True)
                weight = (expd * (1.0 / total)).astype(jnp.bfloat16)
                mixed = jnp.dot(weight, vals, preferred_element_type=jnp.float32)
                for g, h in enumerate(heads):
                    new = wide[:, h * 128 : (h + 1) * 128] + mixed[g * QT : (g + 1) * QT]
                    new = new.astype(jnp.bfloat16)
                    state[layer, rows, h * 128 : (h + 1) * 128] = new
                    new = new.astype(jnp.float32)
                    squares = squares + new * new
            if layer < LAYERS - 1:
                squares = jnp.sum(squares, axis=-1, keepdims=True)
                rs[rows, :] = jnp.broadcast_to(squares, (QT, 128))
            cols = pl.ds(pl.multiple_of(y * WIDE, WIDE), WIDE)

            @pl.when(layer == y)
            def _():
                pltpu.make_async_copy(
                    state.at[layer, rows], out.at[rows, cols], outlocal
                ).start()

            @pl.when(layer != y)
            def _():
                pltpu.make_async_remote_copy(
                    src_ref=state.at[layer, rows],
                    dst_ref=out.at[rows, cols],
                    send_sem=outsend.at[layer],
                    recv_sem=outrecv,
                    device_id=y_id(layer),
                    device_id_type=MESH,
                ).start()

            return 0

        lax.fori_loop(0, REQ, one, 0)
        if layer < LAYERS - 1:
            ssq[layer, y] = rs[...].T[0:8]
            for i in range(1, NY):
                pltpu.make_async_remote_copy(
                    src_ref=ssq.at[layer, y],
                    dst_ref=ssq.at[layer, y],
                    send_sem=qsend.at[layer, i],
                    recv_sem=qrecv.at[layer],
                    device_id=y_id(lax.rem(y + i, NY)),
                    device_id_type=MESH,
                ).start()

    wide = hid[...].astype(jnp.float32)
    mean_sq = jnp.sum(wide * wide, axis=-1, keepdims=True) * (1.0 / D)
    rs[...] = jnp.broadcast_to(lax.rsqrt(mean_sq + 1e-05), (256, 128))
    kv[NRET * PT + QT :] = jnp.zeros((KEYS - NRET * PT - QT, PAIR), jnp.bfloat16)

    for copy in local_copies():
        copy.wait()
    z_first(0)

    def do_step(k):
        if k >= 2:
            x_sent(k - 2)
        choose(k, z)
        for hop in range(1, 5):
            for half in range(2):
                for up in (True, False):
                    if hop <= hops(up, half):
                        z_arrival(k, up, half, hop).wait_recv()
                        if hop < hops(up, half):
                            z_copy(k, up, half, hop + 1).start()
            if hop == 2 and k < LAYERS - 1:
                y_arrived(k + 1)
                z_first(k + 1)
            choose(k, mod(z - hop, NZ))
            if hop < 4:
                choose(k, mod(z + hop, NZ))
            if hop == 3 and k >= 2:
                if k == 2:
                    x_arrived(0)
                    x_arrived(1)
                    attend(0)
                else:
                    x_arrived(2)
                    attend(1)

    for k in range(LAYERS):
        do_step(k)
    x_arrived(3)
    attend(2)
    attend(3)

    x_sent(2)
    x_sent(3)
    for k in range(LAYERS):
        for up in (True, False):
            for half in range(2):
                for hop in range(1, hops(up, half) + 1):
                    z_copy(k, up, half, hop).wait_send()
    for i in range(1, NY):
        for copy in scatter_copies(i):
            copy.wait_send()
        for layer in range(LAYERS - 1):
            what = ssq.at[layer, y]
            pltpu.make_async_copy(what, what, qsend.at[layer, i]).wait()
    for layer in range(LAYERS):

        @pl.when(layer != y)
        def _():
            what = state.at[layer]
            pltpu.make_async_copy(what, what, outsend.at[layer]).wait()

    what = out.at[:, pl.ds(0, 3 * WIDE)]
    pltpu.make_async_copy(what, what, outrecv).wait()
    what = out.at[:, pl.ds(0, WIDE)]
    pltpu.make_async_copy(what, what, outlocal).wait()


def general_attend(store, own, hidden, gain, sel, slots):
    vmem = pl.BlockSpec(memory_space=pltpu.VMEM)
    smem = pl.BlockSpec(memory_space=pltpu.SMEM)
    hbm = pl.BlockSpec(memory_space=pl.ANY)
    bf16 = jnp.bfloat16
    dma = pltpu.SemaphoreType.DMA
    return pl.pallas_call(
        general_kernel,
        out_shape=jax.ShapeDtypeStruct((REQ * QT, D), bf16),
        in_specs=[hbm, hbm, vmem, vmem, smem, smem],
        out_specs=hbm,
        scratch_shapes=[
            pltpu.VMEM((LAYERS, NZ, PASS_DEV, PT, PAIR), bf16),
            pltpu.VMEM((LAYERS, PLANE, NZ, CAP, PT, PAIR), bf16),
            pltpu.VMEM((2, NZ, PLANE, CAP, PT, PAIR), bf16),
            pltpu.VMEM((PLANE * NZ * CAP, PT, PAIR), bf16),
            pltpu.VMEM((PASS_DEV, PT, PAIR), bf16),
            pltpu.VMEM((LAYERS, REQ * QT, PAIR), bf16),
            pltpu.VMEM((KEYS, PAIR), bf16),
            pltpu.VMEM((LAYERS, REQ * QT, WIDE), bf16),
            pltpu.VMEM((REQ * QT, 128), jnp.float32),
            pltpu.VMEM((LAYERS - 1, NY, 8, REQ * QT), jnp.float32),
            dma((NY, 2)),
            dma((LAYERS, 2)),
            dma((NY, 2)),
            dma((LAYERS, 2)),
            dma((4,)),
            dma((LAYERS, 2, 2, 4)),
            dma((LAYERS, 2, 2, 4)),
            dma((LAYERS,)),
            dma((LAYERS,)),
            dma((LAYERS - 1, NY)),
            dma((LAYERS - 1,)),
            dma((LAYERS,)),
            dma(()),
            dma(()),
        ],
        compiler_params=pltpu.CompilerParams(
            collective_id=1, has_side_effects=True, vmem_limit_bytes=60 * 1024 * 1024
        ),
        name="general_attend",
    )(store, own, hidden, gain, sel, slots)


def per_device(hidden, norm_gain, own_kv, passage_kv, retrieval, passage_slot):
    cache, x, y, z, c = where_am_i()
    ids = jnp.broadcast_to(jnp.tile(retrieval.reshape(-1), 4)[None, :], (8, 128))
    rows, gains, tab = greet(ids, passage_slot.reshape(8, 128), norm_gain)
    most_z, most_x = tab[26, 0], tab[27, 0]
    turn = jnp.arange(32, dtype=jnp.int32)

    def fast(cz, collective_id):
        def run(store, own, hidden, gains):
            store = store.reshape(2, PASS_DEV // 2, PT, 4 * HALF * 2)
            return fast_attend(cz, collective_id, store, own, hidden, gains, tab)

        return run

    def general(store, own, hidden, gains):
        gain = lax.dynamic_slice(gains, (0, y * 8, 0), (NY, 8, 128)).reshape(NY, WIDE)
        near = lax.dynamic_slice(rows, (2 * z, 0), (2, 128)).reshape(NC, NX, 32)
        near = near.transpose(1, 0, 2).reshape(PLANE, 32)
        mine = x * NC + c
        owner = near // PASS_DEV
        inside = near % PASS_DEV
        source = (owner // (NZ * NC)) * NC + owner % NC
        plane = (owner // NC) % NZ
        earlier = (owner[:, None, :] == owner[:, :, None]) & (turn[None, :] < turn[:, None])
        rank = jnp.sum(earlier.astype(jnp.int32), axis=2)
        place = jnp.where(source == mine, plane * CAP + rank, -1)
        spots = jnp.arange(NZ * CAP, dtype=jnp.int32)
        sel = jnp.sum(
            jnp.where(place[:, None, :] == spots[None, :, None], inside[:, None, :], 0), axis=2
        )
        sel = sel.reshape(PLANE, NZ, CAP).transpose(1, 0, 2).reshape(NZ, PLANE * CAP)
        slot = (source * NZ + plane) * CAP + rank
        slots = lax.dynamic_slice(slot, (mine, 0), (1, 32)).reshape(32)
        return general_attend(store, own, hidden, gain, sel, slots)

    which = jnp.int32(0)
    for cz in CZS:
        which = which + (most_z > cz).astype(jnp.int32)
    which = jnp.where(most_x > 2 * CX, len(CZS), which)
    branches = [fast(cz, 2 + i) for i, cz in enumerate(CZS)] + [general]
    done = lax.switch(which, branches, passage_kv[0], own_kv[0], hidden, gains)
    return done[None]


def solution(mesh):
    return jax.shard_map(
        per_device,
        mesh=mesh,
        in_specs=(
            P("cache", None),
            P("section", None),
            P("section", "cache", None),
            P("section", "cache", None, None),
            P("cache", None),
            P(),
        ),
        out_specs=P("section", "cache", None),
        check_vma=False,
    )
```

profile of v0, /device:TPU:28, one launch (start us, length us, event | category | flops | bytes accessed | tf_op | source)
XLA Modules:
  0.0 209.4 jit_solution(13844803045882949258)
XLA Ops:
  0.0 0.8 tile.7
  0.8 0.1 broadcast_in_dim.48
  0.9 0.6 broadcast_in_dim.49.ids_ref
  1.5 16.1 %greet.1 = (s32[16,128]{1,0:T(8,128)S(1)}, f32[4,32,128]{2,1,0:T(8,128)S(1)}, s32[32,128]{1,0:T(8,128)S(1)}) custom-call(s32[8,128]{1,0:T(8,128)} %broadcast_in_dim.49.ids_ref, s32[8,128]{1,0:T(8,128)} %bitcast.37, bf16[1,4096]{1,0:T(2,128)(2,1)} %gain_ref.1), custom_call_target="tpu_custom_call" | custom-call | tf_op jit(solution)/shard_map/greet/pallas_call | solution.py:236
  17.6 0.5 fusion.9
  20.1 188.0 %conditional.1 = (bf16[1,256,4096]{2,1,0:T(8,128)(2,1)S(1)}) conditional(s32[]{:T(128)} %bitcast.14, (bf16[1,16,32,2048]{3,2,1,0:T(8,128)(2,1)}, bf16[256,2048]{1,0:T(8,128)(2,1)}, bf16[256,4096]{1,0:T(8,128)(2,1)}, f32[4,32,128]{2,1,0:T(8,128)S(1)}, s32[32,128]{1,0:T(8,128)S(1)}) %tuple.41, (bf16[1,16,32,2048]{3,2,1,0:T(8,128)(2,1)}, ...), branch_computations={%region_0.1_spmd, %region_1.2_spmd, %region_2.5_spmd} | conditional | flops 67239 | bytes 89396 | solution.py:1212
  20.1 187.8 %fast_attend_12.1 = bf16[256,4096]{1,0:T(8,128)(2,1)S(1)} custom-call(bf16[2,8,32,2048]{3,2,1,0:T(8,128)(2,1)} %bitcast.22, bf16[256,2048]{1,0:T(8,128)(2,1)} %get-tuple-element.210.own_in, bf16[256,4096]{1,0:T(8,128)(2,1)} %get-tuple-element.211.hid, f32[4,32,128]{2,1,0:T(8,128)S(1)} %get-tuple-element.212.gain, s32[32,128]{1,0:T(8,128)S(1)} %get-tuple-element.213.tab), custom_call_target="tpu_custom_call" | custom-call | tf_op jit(solution)/shard_map/cond/branch_0_fun/fast_attend_12/pallas_call | solution.py:736
  208.1 1.3 copy.28
  (2 shorter events, 0.0 us)
where the time goes:
time: 210 us; the launch traced here: 209 us
  Pallas kernels  204 us (97%)
  local copies, waits for them, and re-layouts  3.32 us (2%)
    pallas_call x1, Pallas kernels, fast_attend(): pl.pallas_call(functools.partial(fast_kernel, cz), out_shape=jax.ShapeDty...  188 us
    pallas_call x1, Pallas kernels, greet(): pl.pallas_call(greet_kernel, out_shape=(jax.ShapeDtypeStruct((2 * NZ, 128...  16.1 us

commit v1 on v0

--- a/solution.py
+++ b/solution.py
@@ -24,7 +24,7 @@
 MESH = pl.DeviceIdType.MESH
 STEPS = 2 * LAYERS
 ONE = 256
-CZS = (12, 14)
+CZS = (11, 13)
 CX = 8
 OWN = 64
 KV_ROWS = NRET * PT + OWN
@@ -162,70 +162,80 @@
     inside = rows % PASS_DEV
     plane = (owner // NC) % NZ
     o8 = (owner % NC) * NX + owner // (NZ * NC)
-    stripe = (inside + o8) % PLANE
-    place = o8 * 2 + inside // PLANE
-    group = plane * PLANE + stripe
-    chip = stripe % NX
+    number = o8 * PASS_DEV + inside
 
     wide = (128, 128)
+    count = jnp.zeros((NZ, 128), f32)
+    for i in range(2 * NZ):
+        in_plane = jnp.broadcast_to(plane[i : i + 1], (NZ, 128)) == subs((NZ, 128))
+        is_number = jnp.broadcast_to(number[i : i + 1], wide) == subs(wide)
+        count = count + lax.dot_general(
+            in_plane.astype(f32).astype(bf16),
+            is_number.astype(f32).astype(bf16),
+            (((1,), (1,)), ((), ())),
+            preferred_element_type=f32,
+        )
+    need = (count > 0.5).astype(f32)
+    before = mm(need, (subs(wide) < lanes(wide)).astype(f32))
+    first_of = mm(before, (subs(wide) == lanes(wide) // PASS_DEV * PASS_DEV).astype(f32))
+    for i in range(2 * NZ):
+        in_plane = jnp.broadcast_to(plane[i : i + 1], (NZ, 128)) == subs((NZ, 128))
+        is_number = jnp.broadcast_to(number[i : i + 1], wide) == subs(wide)
+        found = mm(before, is_number.astype(f32)) * in_plane.astype(f32)
+        fields[0, i : i + 1, :] = jnp.sum(found, axis=0, keepdims=True).astype(i32)
+    place = fields[0]
+    chip = (place % PLANE) % NX
+
     same = (subs(wide) // 32 == lanes(wide) // 32) & (subs(wide) < lanes(wide))
     rank = jnp.zeros((2 * NZ, 128), f32)
     for v in range(NX):
         here = (chip == v).astype(f32)
         rank = rank + here * mm(here, same.astype(f32))
     rank = rank.astype(i32)
-    fields[0] = group
-    fields[1] = place
-    fields[2] = chip
-    fields[3] = rank
-
-    groups = NZ * PLANE
-    count = jnp.zeros((PASS_DEV, groups), f32)
-    for i in range(2 * NZ):
-        in_group = jnp.broadcast_to(group[i : i + 1], (groups, 128)) == subs((groups, 128))
-        in_place = jnp.broadcast_to(place[i : i + 1], (PASS_DEV, 128)) == subs((PASS_DEV, 128))
-        count = count + lax.dot_general(
-            in_place.astype(f32).astype(bf16),
-            in_group.astype(f32).astype(bf16),
-            (((1,), (1,)), ((), ())),
-            preferred_element_type=f32,
-        )
-    need = (count > 0.5).astype(f32)
-    square = (PASS_DEV, PASS_DEV)
-    before = mm((lanes(square) < subs(square)).astype(f32), need)
+    fields[1] = plane
+    fields[2] = rank
 
     def one_max(value):
         return jnp.max(jnp.max(value, axis=1, keepdims=True), axis=0, keepdims=True)
 
-    most_z = one_max(jnp.sum(need, axis=0, keepdims=True)).astype(i32)
+    most_z = one_max(jnp.sum(need, axis=1, keepdims=True)).astype(i32)
     most_x = one_max(rank) + 1
 
-    ours = (lanes((PASS_DEV, groups)) == z * PLANE + me).astype(f32)
-    my_need = jnp.sum(need * ours, axis=1, keepdims=True)
-    my_before = jnp.sum(before * ours, axis=1, keepdims=True).astype(i32)
-    hit = (my_before == lanes((PASS_DEV, 128))) & (my_need > 0.5)
-    csel = jnp.sum(jnp.where(hit, subs((PASS_DEV, 128)), 0), axis=0, keepdims=True)
-    tab_out[0:8, :] = jnp.broadcast_to(csel, (8, 128))
+    ours = (subs((NZ, 128)) == z).astype(f32)
+    my_need = jnp.sum(need * ours, axis=0, keepdims=True) > 0.5
+    my_rank = jnp.sum(before * ours, axis=0, keepdims=True).astype(i32)
+    my_first = jnp.sum(first_of * ours, axis=0, keepdims=True).astype(i32)
+    again = (my_rank - my_first) // PLANE
+    lane = lanes((1, 128))
+    tall = (PASS_DEV, 128)
+    key = jnp.where(my_need & (lane // PASS_DEV == me), my_rank % PLANE * 2 + again, -1)
+    hit = jnp.broadcast_to(key, tall) == subs(tall)
+    ssel = jnp.sum(jnp.where(hit, lanes(tall) % PASS_DEV, 0), axis=1, keepdims=True)
+    key = jnp.where(my_need & (my_rank % PLANE == me), my_rank // PLANE, -1)
+    hit = jnp.broadcast_to(key, tall) == subs(tall)
+    spot = jnp.broadcast_to(lane // PASS_DEV * 2 + again, tall)
+    csel = jnp.sum(jnp.where(hit, spot, 0), axis=1, keepdims=True)
+    tab_out[0:16, :] = jnp.where(
+        lanes(tall) == 0, jnp.broadcast_to(csel, tall), jnp.broadcast_to(ssel, tall)
+    )
 
     block = (subs(wide) // 32 == lanes(wide)).astype(f32)
     for half in range(2):
         at = pl.ds(2 * z + half, 1)
-        g, a, b, k = fields[0, at, :], fields[1, at, :], fields[2, at, :], fields[3, at, :]
-        in_group = jnp.broadcast_to(g, (groups, 128)) == subs((groups, 128))
-        in_place = jnp.broadcast_to(a, (PASS_DEV, 128)) == subs((PASS_DEV, 128))
-        spot = mm(before, in_group.astype(f32)) * in_place.astype(f32)
-        spot = jnp.sum(spot, axis=0, keepdims=True)
-        core = (g % PLANE) // NX
-        where = ((core * NZ + g // PLANE) * CZS[-1]).astype(f32) + jnp.minimum(spot, CZS[-1] - 1.0)
+        g, p, k = fields[0, at, :], fields[1, at, :], fields[2, at, :]
+        t = g % PLANE
+        b = t % NX
+        where = ((t // NX) * NZ + p) * CZS[-1] + jnp.minimum(g // PLANE, CZS[-1] - 1)
+        where = where.astype(f32)
         key = jnp.where((b == x) & (k % NC == c), k // NC, -1)
         hit = jnp.broadcast_to(key, (CX, 128)) == subs((CX, 128))
         chosen = jnp.where(hit, jnp.broadcast_to(where, (CX, 128)), 0.0)
-        tab_out[8 + 8 * half : 16 + 8 * half, :] = mm(chosen, block).astype(i32)
+        tab_out[16 + 8 * half : 24 + 8 * half, :] = mm(chosen, block).astype(i32)
         slot = ((k % NC) * NX + b) * CX + jnp.minimum(k // NC, CX - 1)
-        tab_out[24 + half : 25 + half, :] = slot
-    tab_out[26:27, :] = jnp.broadcast_to(most_z, (1, 128))
-    tab_out[27:28, :] = jnp.broadcast_to(most_x, (1, 128))
-    tab_out[28:32, :] = jnp.zeros((4, 128), i32)
+        tab_out[32 + half : 33 + half, :] = slot
+    tab_out[34:35, :] = jnp.broadcast_to(most_z, (1, 128))
+    tab_out[35:36, :] = jnp.broadcast_to(most_x, (1, 128))
+    tab_out[36:40, :] = jnp.zeros((4, 128), i32)
     for copy in second:
         copy.wait()
 
@@ -238,7 +248,7 @@
         out_shape=(
             jax.ShapeDtypeStruct((2 * NZ, 128), jnp.int32),
             jax.ShapeDtypeStruct((NY, 32, 128), jnp.float32),
-            jax.ShapeDtypeStruct((32, 128), jnp.int32),
+            jax.ShapeDtypeStruct((40, 128), jnp.int32),
         ),
         in_specs=[vmem, vmem, vmem],
         out_specs=(vmem, vmem, vmem),
@@ -247,7 +257,7 @@
             pltpu.VMEM((PLANE, 8, 128), jnp.int32),
             pltpu.VMEM((8, 128), jnp.int32),
             pltpu.VMEM((NZ, 8, 128), jnp.int32),
-            pltpu.VMEM((4, 2 * NZ, 128), jnp.int32),
+            pltpu.VMEM((3, 2 * NZ, 128), jnp.int32),
             dma((PLANE,)),
             dma((PLANE,)),
             dma((NZ,)),
@@ -262,7 +272,7 @@
 
 def fast_kernel(
     cz, store, own_in, hid, gain, tab, out, ybuf, send, kvs, own, state, staged, gains, rs,
-    ssq, box, packed, ysend, yrecv, osend, orecv, local, ssend, srecv, csend, crecv, zsend, zrecv, xsend, xrecv,
+    ssq, box, ystage, sbox, packed, ysend, yrecv, osend, orecv, local, ssend, srecv, csend, crecv, zsend, zrecv, xsend, xrecv,
     qsend, qrecv, outsend, outrecv, outlocal, *many
 ):
     strips, pools, recvs = many[:STEPS], many[STEPS : 2 * STEPS], many[2 * STEPS :]
@@ -305,8 +315,8 @@
                 cols = pl.ds(pl.multiple_of(part * 1024 + y * HALF + j * 128, 128), 128)
                 made.append(
                     pltpu.make_async_copy(
-                        store.at[:, :, :, cols],
-                        ybuf.at[step_of(2 * y + j, y), :, :, :, pl.ds(part * 128, 128)],
+                        store.at[:, :, cols],
+                        ybuf.at[step_of(2 * y + j, y), :, :, pl.ds(part * 128, 128)],
                         local.at[2 * j + part],
                     )
                 )
@@ -326,8 +336,8 @@
             cols = pl.ds(pl.multiple_of(part * 1024 + s * HALF + j * 128, 128), 128)
             made.append(
                 pltpu.make_async_copy(
-                    store.at[:, :, :, cols],
-                    box.at[i - 1, j, :, :, :, pl.ds(part * 128, 128)],
+                    store.at[:, :, cols],
+                    box.at[i - 1, j, :, :, pl.ds(part * 128, 128)],
                     packed.at[i, j, part],
                 )
             )
@@ -363,10 +373,21 @@
         return made
 
     def stripe(q):
+        par = q % 2
+        if q >= 2:
+            striped(q - 2)
+        ystage[...] = ybuf[q]
+
+        def fill(i, _):
+            sbox[par, i] = ystage[tab[i, 1]]
+            return 0
+
+        lax.fori_loop(0, 2 * PLANE, fill, 0)
+
         def push(i, _):
             t = lax.rem(me + i, PLANE)
             pltpu.make_async_remote_copy(
-                src_ref=ybuf.at[q, :, mod(t - me, PLANE)],
+                src_ref=sbox.at[par, pl.ds(t * 2, 2)],
                 dst_ref=strips[q].at[pl.ds(me * 2, 2)],
                 send_sem=ssend.at[q],
                 recv_sem=srecv.at[q],
@@ -375,8 +396,12 @@
             ).start()
             return 0
 
-        strips[q][pl.ds(me * 2, 2)] = ybuf[q, :, 0]
+        strips[q][pl.ds(me * 2, 2)] = sbox[par, pl.ds(me * 2, 2)]
         lax.fori_loop(1, PLANE, push, 0)
+
+    def striped(q):
+        what = strips[q].at[pl.ds(0, 2 * PLANE - 2)]
+        pltpu.make_async_copy(what, what, ssend.at[q]).wait()
 
     def z_ref(q, plane, half):
         at = (c * NZ + plane) * CZS[-1]
@@ -423,7 +448,7 @@
         what = strips[q].at[pl.ds(0, 2 * PLANE - 2)]
         pltpu.make_async_copy(what, what, srecv.at[q]).wait()
         for i in range(cz):
-            pools[q][(c * NZ + z) * CZS[-1] + i] = strips[q][tab[0, i]]
+            pools[q][(c * NZ + z) * CZS[-1] + i] = strips[q][tab[i, 0]]
         for half in range(2):
             for up in (True, False):
                 z_copy(q, up, half, 1).start()
@@ -438,7 +463,7 @@
 
         def fill(t, _):
             for i in range(CX):
-                send[par, t, i] = pools[q][tab[8 + 8 * (t // 4) + i, lax.rem(t, 4)]]
+                send[par, t, i] = pools[q][tab[16 + 8 * (t // 4) + i, lax.rem(t, 4)]]
             return 0
 
         lax.fori_loop(0, PLANE, fill, 0)
@@ -469,7 +494,7 @@
 
         def one(r, _):
             for n in range(NRET):
-                at = tab[24 + me // 4, lax.rem(me, 4) * 32 + r * NRET + n]
+                at = tab[32 + me // 4, lax.rem(me, 4) * 32 + r * NRET + n]
                 kvs[part, r, n * PT : (n + 1) * PT] = recvs[q][at]
             return 0
 
@@ -695,11 +720,11 @@
     assemble(STEPS - 1)
     attend_rows(3, 0, REQ, 2, (1,))
 
+    striped(STEPS - 2)
+    striped(STEPS - 1)
     x_sent(STEPS - 2)
     x_sent(STEPS - 1)
     for q in range(STEPS):
-        what = strips[q].at[pl.ds(0, 2 * PLANE - 2)]
-        pltpu.make_async_copy(what, what, ssend.at[q]).wait()
         what = pools[q].at[pl.ds(0, NZ * cz)]
         pltpu.make_async_copy(what, what, csend.at[q]).wait()
         for up in (True, False):
@@ -739,7 +764,7 @@
         in_specs=[hbm, hbm, vmem, vmem, smem],
         out_specs=hbm,
         scratch_shapes=[
-            pltpu.VMEM((STEPS, 2, PLANE, PT, ONE), bf16),
+            pltpu.VMEM((STEPS, PASS_DEV, PT, ONE), bf16),
             pltpu.VMEM((2, PLANE, CX, PT, ONE), bf16),
             pltpu.VMEM((STEPS, REQ, NRET * PT, ONE), bf16),
             pltpu.VMEM((LAYERS, REQ * QT, PAIR), bf16),
@@ -748,7 +773,9 @@
             pltpu.VMEM((LAYERS, 2, 128, 4 * QT), jnp.float32),
             pltpu.VMEM((8, 4 * QT), jnp.float32),
             pltpu.VMEM((LAYERS - 1, NY, 8, 4 * QT), jnp.float32),
-            pltpu.VMEM((NY - 1, 2, 2, PLANE, PT, ONE), bf16),
+            pltpu.VMEM((NY - 1, 2, PASS_DEV, PT, ONE), bf16),
+            pltpu.VMEM((PASS_DEV, PT, ONE), bf16),
+            pltpu.VMEM((2, 2 * PLANE, PT, ONE), bf16),
             dma((NY, 2, 2)),
             dma((NY, 2)),
             dma((STEPS,)),
@@ -1173,12 +1200,11 @@
     cache, x, y, z, c = where_am_i()
     ids = jnp.broadcast_to(jnp.tile(retrieval.reshape(-1), 4)[None, :], (8, 128))
     rows, gains, tab = greet(ids, passage_slot.reshape(8, 128), norm_gain)
-    most_z, most_x = tab[26, 0], tab[27, 0]
+    most_z, most_x = tab[34, 0], tab[35, 0]
     turn = jnp.arange(32, dtype=jnp.int32)
 
     def fast(cz, collective_id):
         def run(store, own, hidden, gains):
-            store = store.reshape(2, PASS_DEV // 2, PT, 4 * HALF * 2)
             return fast_attend(cz, collective_id, store, own, hidden, gains, tab)
 
         return run
@@ -1206,7 +1232,7 @@
 
     which = jnp.int32(0)
     for cz in CZS:
-        which = which + (most_z > cz).astype(jnp.int32)
+        which = which + (most_z > PLANE * cz).astype(jnp.int32)
     which = jnp.where(most_x > 2 * CX, len(CZS), which)
     branches = [fast(cz, 2 + i) for i, cz in enumerate(CZS)] + [general]
     done = lax.switch(which, branches, passage_kv[0], own_kv[0], hidden, gains)

time: 210 us -> 207 us (0.986)
  Pallas kernels: 204 us -> 200 us
    pallas_call x1, Pallas kernels: 188 us -> 184 us  [fast_attend(): pl.pallas_call(functools.partial(fast_kernel, cz), out_shape=jax.ShapeDty...]
where the time goes in v1:
time: 207 us; the launch traced here: 206 us
  Pallas kernels  200 us (97%)
  local copies, waits for them, and re-layouts  3.32 us (2%)
    pallas_call x1, Pallas kernels, fast_attend(): pl.pallas_call(functools.partial(fast_kernel, cz), out_shape=jax.ShapeDty...  184 us
    pallas_call x1, Pallas kernels, greet(): pl.pallas_call(greet_kernel, out_shape=(jax.ShapeDtypeStruct((2 * NZ, 128...  16.7 us

profile of v1, /device:TPU:28, one launch (start us, length us, event | category | flops | bytes accessed | tf_op | source)
XLA Modules:
  0.0 205.9 jit_solution(6153226464465623292)
XLA Ops:
  0.0 0.8 tile.7
  0.8 0.1 broadcast_in_dim.48
  0.9 0.6 broadcast_in_dim.49.ids_ref
  1.5 16.7 %greet.1 = (s32[16,128]{1,0:T(8,128)S(1)}, f32[4,32,128]{2,1,0:T(8,128)S(1)}, s32[40,128]{1,0:T(8,128)S(1)}) custom-call(s32[8,128]{1,0:T(8,128)} %broadcast_in_dim.49.ids_ref, s32[8,128]{1,0:T(8,128)} %bitcast.35, bf16[1,4096]{1,0:T(2,128)(2,1)} %gain_ref.1), custom_call_target="tpu_custom_call" | custom-call | tf_op jit(solution)/shard_map/greet/pallas_call | solution.py:246
  18.2 0.5 fusion.9
  20.7 183.9 %conditional.1 = (bf16[1,256,4096]{2,1,0:T(8,128)(2,1)S(1)}) conditional(s32[]{:T(128)} %bitcast.11, (bf16[16,32,2048]{2,1,0:T(8,128)(2,1)}, bf16[256,2048]{1,0:T(8,128)(2,1)}, bf16[256,4096]{1,0:T(8,128)(2,1)}, f32[4,32,128]{2,1,0:T(8,128)S(1)}, s32[40,128]{1,0:T(8,128)S(1)}) %tuple.44, (bf16[16,32,2048]{2,1,0:T(8,128)(2,1)}, ...), branch_computations={%region_0.1_spmd, %region_1.2_spmd, %region_2.5_spmd} | conditional | flops 67241 | bytes 89420 | solution.py:1238
  20.7 183.7 %fast_attend_11.1 = bf16[256,4096]{1,0:T(8,128)(2,1)S(1)} custom-call(bf16[16,32,2048]{2,1,0:T(8,128)(2,1)} %get-tuple-element.205.store, bf16[256,2048]{1,0:T(8,128)(2,1)} %get-tuple-element.206.own_in, bf16[256,4096]{1,0:T(8,128)(2,1)} %get-tuple-element.207.hid, f32[4,32,128]{2,1,0:T(8,128)S(1)} %get-tuple-element.208.gain, ...), custom_call_target="tpu_custom_call" | custom-call | tf_op jit(solution)/shard_map/cond/branch_0_fun/fast_attend_11/pallas_call | solution.py:761
  204.6 1.3 copy.28
  (2 shorter events, 0.0 us)
